TPU v7x, 32 devices: a whole 2x2x4 slice. The times are simulated.
32 devices in a mesh: groups: 2 (over y), tenant: 4 (over x, core), tensor: 4 (over z).
Axes of the slice: x: 2, y: 2, z: 4, core: 2. Of those that a mesh axis runs over, the one named last changes fastest.
Arguments:
- feats: bfloat16 [1024, 8192], P(('groups', 'tenant'), 'tensor'), parts along dimension 0, may hold values from -6 to 6
- gate_preactivation: bfloat16 [1024, 14784], P(('groups', 'tenant'), 'tensor'), parts along dimension 0, may hold values from -8 to 8
- row_loss_curvature: bfloat16 [1024], P(('groups', 'tenant')), parts along dimension 0, may hold values from 0.25 to 4
- row_adapter_index: int32 [1024], P(('groups', 'tenant')), parts along dimension 0, may hold values from 0 to 15, as said below
- row_adapter_position: int32 [1024], P(('groups', 'tenant')), parts along dimension 0, may hold values from 0 to 31, as said below
- down_projection_weight: bfloat16 [14784, 8192], P('tensor'), may hold values from -0.0625 to 0.0625
- adapter_input_factors: bfloat16 [32, 8192, 32], P(('groups', 'tenant'), 'tensor'), parts along dimension 0, may hold values from -6 to 6
- adapter_output_factors: bfloat16 [32, 32, 14784], P(('groups', 'tenant'), None, 'tensor'), parts along dimension 0, may hold values from -6 to 6
- iterate_input_factors: float32 [32, 8192, 32], P(('groups', 'tenant'), 'tensor'), parts along dimension 0, may hold values from -6 to 6
- iterate_output_factors: float32 [32, 32, 14784], P(('groups', 'tenant'), None, 'tensor'), parts along dimension 0, may hold values from -6 to 6
- input_factor_gradient: float32 [32, 8192, 32], P(('groups', 'tenant'), 'tensor'), parts along dimension 0, may hold values from -6 to 6
- output_factor_gradient: float32 [32, 32, 14784], P(('groups', 'tenant'), None, 'tensor'), parts along dimension 0, may hold values from -6 to 6
Outputs:
- new_a: float32 [32, 8192, 32], P(('groups', 'tenant'), 'tensor'), parts along dimension 0
- new_b: float32 [32, 32, 14784], P(('groups', 'tenant'), None, 'tensor'), parts along dimension 0
- row_cot: bfloat16 [1024, 8192], P(('groups', 'tenant'), 'tensor'), parts along dimension 0
There are 2 independent parts, one for each index of `groups`. A program takes and returns all parts, laid end to end along the dimension named above; an argument that names none is the same for every part. Nothing has to cross between parts.
Inputs may be any that keep to these rules, and one draw needn't show every extreme that they name: `row_adapter_index`: every device of the tenant axis holds exactly 8 rows of each adapter. `row_adapter_position`: the rows of one adapter carry each slot exactly once.
All inputs are finite; a program needn't handle non-finite values.
Results may differ from a plain program's by a relative error of at most 0.0053.
Values may be sent and summed in bfloat16 or wider, within the bound.
A program may use at most 192 MiB of HBM per device.

v0:
```python
import math

import jax
import jax.numpy as jnp
from jax import lax
from jax.sharding import PartitionSpec as P

MODEL_WIDTH = 8192
ADAPTER_RANK = 32


damping = 0.05
lissa_scale = 2.0


def shards(
    feats,
    gate_preactivation,
    row_loss_curvature,
    row_adapter_index,
    row_adapter_position,
    down_projection_weight,
    adapter_input_factors,
    adapter_output_factors,
    iterate_input_factors,
    iterate_output_factors,
    input_factor_gradient,
    output_factor_gradient,
):
    highest_precision = lax.Precision.HIGHEST
    tenant_count = lax.axis_size("tenant")
    local_tenant_count = adapter_input_factors.shape[0]
    row_count = feats.shape[0]
    rows_each = row_count // local_tenant_count
    per_dest = row_count // tenant_count
    d_local = feats.shape[1]
    f_local = gate_preactivation.shape[1]
    target = row_adapter_index // local_tenant_count
    matches = (target[:, None] == jnp.arange(tenant_count, dtype=jnp.int32)[None, :]).astype(
        jnp.int32
    )
    within = jnp.sum((jnp.cumsum(matches, axis=0) - 1) * matches, axis=1)
    send_pos = target * per_dest + within
    send_order = (
        jnp.zeros((row_count,), jnp.int32).at[send_pos].set(jnp.arange(row_count, dtype=jnp.int32))
    )
    place_local = row_adapter_index % local_tenant_count * rows_each + row_adapter_position
    got_x, got_gate, got_weight = (
        lax.all_to_all(feats[send_order], "tenant", split_axis=0, concat_axis=0, tiled=True),
        lax.all_to_all(
            gate_preactivation[send_order], "tenant", split_axis=0, concat_axis=0, tiled=True
        ),
        lax.all_to_all(
            row_loss_curvature[send_order], "tenant", split_axis=0, concat_axis=0, tiled=True
        ),
    )
    arrival = lax.all_to_all(
        place_local[send_order], "tenant", split_axis=0, concat_axis=0, tiled=True
    )
    grouped_input_rows = jnp.zeros_like(got_x).at[arrival].set(got_x)
    grouped_gate = jnp.zeros_like(got_gate).at[arrival].set(got_gate)
    weights = jnp.zeros_like(got_weight).at[arrival].set(got_weight).astype(jnp.float32)
    input_three_axes = grouped_input_rows.reshape(local_tenant_count, rows_each, d_local)
    x_float = input_three_axes.astype(jnp.float32)
    partial_product = jnp.einsum(
        "ake,aex->akx", input_three_axes, adapter_input_factors, preferred_element_type=jnp.float32
    )
    part_q = jnp.einsum("ake,aex->akx", x_float, iterate_input_factors, precision=highest_precision)
    summed_p, summed_q = lax.psum((partial_product, part_q), "tensor")
    project_rows = summed_p / math.sqrt(MODEL_WIDTH)
    lowrank_tangent = summed_q / math.sqrt(MODEL_WIDTH)
    up_tangent = (
        jnp.einsum(
            "wqh,whx->wqx",
            lowrank_tangent,
            adapter_output_factors.astype(jnp.float32),
            precision=highest_precision,
        )
        + jnp.einsum(
            "wqh,whx->wqx", project_rows, iterate_output_factors, precision=highest_precision
        )
    ) / math.sqrt(ADAPTER_RANK)
    gate_act = jax.nn.silu(grouped_gate.astype(jnp.float32)).reshape(
        local_tenant_count, rows_each, f_local
    )
    hidden_tan = (gate_act * up_tangent).astype(jnp.bfloat16).reshape(row_count, f_local)
    out_tan = jnp.dot(hidden_tan, down_projection_weight, preferred_element_type=jnp.float32)
    out_share = lax.psum_scatter(out_tan, "tensor", scatter_dimension=1, tiled=True)
    row_cot = (weights[:, None] * out_share).astype(jnp.bfloat16)
    hidden_bar = lax.dot_general(
        lax.all_gather(row_cot, "tensor", axis=1, tiled=True),
        down_projection_weight,
        (((1,), (1,)), ((), ())),
        preferred_element_type=jnp.float32,
    )
    up_cotangent = (gate_act * hidden_bar.reshape(local_tenant_count, rows_each, f_local)).astype(
        jnp.bfloat16
    )
    partial_backward = jnp.einsum(
        "acv,apv->acp", up_cotangent, adapter_output_factors, preferred_element_type=jnp.float32
    )
    lowrank_backward = lax.psum(partial_backward, "tensor") / math.sqrt(ADAPTER_RANK)
    curve_a = jnp.einsum(
        "tsd,tsr->tdr", x_float, lowrank_backward, precision=highest_precision
    ) / math.sqrt(MODEL_WIDTH)
    curvature_output_factor = jnp.einsum(
        "bji,bjw->biw", project_rows, up_cotangent.astype(jnp.float32), precision=highest_precision
    ) / math.sqrt(ADAPTER_RANK)
    new_a = input_factor_gradient + (1.0 - damping) * iterate_input_factors - curve_a / lissa_scale
    new_b = (
        output_factor_gradient
        + (1.0 - damping) * iterate_output_factors
        - curvature_output_factor / lissa_scale
    )
    return (new_a, new_b, row_cot)


def solution(mesh):
    placed = (
        P(("groups", "tenant"), "tensor"),
        P(("groups", "tenant"), "tensor"),
        P(("groups", "tenant")),
        P(("groups", "tenant")),
        P(("groups", "tenant")),
        P("tensor", None),
        P(("groups", "tenant"), "tensor", None),
        P(("groups", "tenant"), None, "tensor"),
        P(("groups", "tenant"), "tensor", None),
        P(("groups", "tenant"), None, "tensor"),
        P(("groups", "tenant"), "tensor", None),
        P(("groups", "tenant"), None, "tensor"),
    )
    return jax.shard_map(
        shards,
        mesh=mesh,
        in_specs=placed,
        out_specs=(
            P(("groups", "tenant"), "tensor", None),
            P(("groups", "tenant"), None, "tensor"),
            P(("groups", "tenant"), "tensor"),
        ),
        check_vma=False,
    )
```

profile of v0, /device:TPU:0, one launch (start us, length us, event | category | flops | bytes accessed | tf_op | source)
XLA Modules:
  0.0 284.5 jit_solution(9089982798775462545)
XLA Ops:
  11.3 4.2 %all-to-all-start = ((s32[4,32,1]{1,2,0:T(1,128)}), s32[4,32,1]{1,2,0:T(1,128)S(1)}, u32[]{:S(2)}, u32[]{:S(2)}) async-start(s32[4,32,1]{1,2,0:T(1,128)} %bitcast), calls=%async_computation | async-start | bytes 4096 | tf_op jit(solution)/shard_map/all_to_all | solution.py:57
  15.6 1.7 gather_fusion.1
  17.3 1.9 all-to-all-done
  19.2 3.5 %all-to-all-start.1 = ((bf16[4,32,2048]{2,1,0:T(8,128)(2,1)}), bf16[4,32,2048]{2,1,0:T(8,128)(2,1)S(1)}, u32[]{:S(2)}, u32[]{:S(2)}) async-start(bf16[4,32,2048]{2,1,0:T(8,128)(2,1)} %bitcast.2), calls=%async_computation.1 | async-start | bytes 1048576 | tf_op jit(solution)/shard_map/all_to_all | solution.py:49
  23.9 2.1 gather_fusion.2
  27.3 4.3 %all-to-all-done.1 = bf16[4,32,2048]{2,1,0:T(8,128)(2,1)S(1)} async-done(((bf16[4,32,2048]{2,1,0:T(8,128)(2,1)}), bf16[4,32,2048]{2,1,0:T(8,128)(2,1)S(1)}, u32[]{:S(2)}, u32[]{:S(2)}) %all-to-all-start.1) | async-done | bytes 524320 | tf_op jit(solution)/shard_map/all_to_all | solution.py:49
  32.3 3.5 %all-to-all-start.2 = ((bf16[4,32,3696]{2,1,0:T(8,128)(2,1)}), bf16[4,32,3696]{2,1,0:T(8,128)(2,1)S(1)}, u32[]{:S(2)}, u32[]{:S(2)}) async-start(bf16[4,32,3696]{2,1,0:T(8,128)(2,1)} %bitcast.5), calls=%async_computation.2 | async-start | bytes 1900544 | tf_op jit(solution)/shard_map/all_to_all | solution.py:50
  35.9 2.0 scatter_custom_fusion.1
  37.9 2.0 fusion.34
  41.1 22.5 %all-reduce = (f32[4,32,32]{2,1,0:T(8,128)S(1)}, f32[4,32,32]{2,1,0:T(8,128)S(1)}) all-reduce(f32[4,32,32]{2,1,0:T(8,128)} %fusion.33, f32[4,32,32]{2,1,0:T(8,128)} %fusion.34), channel_id=1, replica_groups=mesh['groups'=2,'tenant'=4,'tensor'=4] {'tensor'}, use_global_device_ids=true, to_apply=%region_6.7 | all-reduce | flops 8192 | bytes 65536 | tf_op jit(solution)/shard_map/psum | solution.py:69
  63.7 2.1 fusion.13
  65.8 2.9 %scatter_custom_fusion.2 = bf16[128,3696]{1,0:T(8,128)(2,1)} fusion(s32[128]{0:T(128)S(1)} %fusion.24, bf16[128,3696]{1,0:T(8,128)(2,1)S(1)} %bitcast.37, bf16[]{:T(256)} %constant.56.clone.1), kind=kCustom, calls=%fused_computation.23 | custom fusion | bytes 946178 | tf_op jit(solution)/shard_map/scatter | solution.py:61
  68.7 1.8 convert_multiply_fusion
  70.5 3.4 %fusion.3 = bf16[4,32,3696]{2,1,0:T(8,128)(2,1)S(1)} fusion(f32[4,32,3696]{2,1,0:T(8,128)S(1)} %bitcast.30, f32[4,32,3696]{2,1,0:T(8,128)} %fusion.13, f32[4,32,3696]{2,1,0:T(8,128)S(1)} %copy-done.4, f32[4,32,32]{2,1,0:T(8,128)S(1)} %get-tuple-element.4), kind=kOutput, calls=%fused_computation.13 | convolution fusion | flops 183562240 | bytes 6639616 | tf_op jit(solution)/shard_map/wqh,whx->wqx/dot_general | solution.py:79
  73.9 23.6 %fusion.35 = f32[128,8192]{1,0:T(8,128)} fusion(bf16[128,3696]{1,0:T(8,128)(2,1)S(1)} %bitcast.36, bf16[3696,8192]{1,0:T(8,128)(2,1)} %param.17), kind=kOutput, calls=%fused_computation.61 | convolution fusion | flops 7751073792 | bytes 65695744 | tf_op jit(solution)/shard_map/dot_general | solution.py:87
  99.5 6.5 %all_to_all.49 = bf16[4,32,1]{1,2,0:T(2,128)(2,1)S(1)} all-to-all(bf16[4,32,1]{1,2,0:T(2,128)(2,1)S(1)} %all_to_all.44), channel_id=1, replica_groups=mesh['groups'=2,'tenant'=4,'tensor'=4] {'tenant'}, dimensions={0} | all-to-all | bytes 512 | tf_op jit(solution)/shard_map/all_to_all | solution.py:53
  107.4 65.5 %reduce-scatter.2.cloned.1.call-done = f32[128,2048]{1,0:T(8,128)} async-done(((f32[128,8192]{1,0:T(8,128)}), f32[128,2048]{1,0:T(8,128)}) %reduce-scatter.2.cloned.1.call-update) | async-done | bytes 1048592 | tf_op jit(solution)/shard_map/reduce_scatter | solution.py:88
  173.0 2.1 multiply_convert_fusion.1
  175.2 46.6 %all-gather.2.cloned.1.call-done = bf16[128,8192]{1,0:T(8,128)(2,1)} async-done(((bf16[128,2048]{1,0:T(8,128)(2,1)}), bf16[128,8192]{1,0:T(8,128)(2,1)}) %all-gather.2.cloned.1.call-update) | async-done | bytes 2097168 | tf_op jit(solution)/shard_map/all_gather | solution.py:91
  221.8 27.9 %fusion.36 = f32[128,3696]{1,0:T(8,128)} fusion(bf16[128,8192]{1,0:T(8,128)(2,1)} %all-gather.2.cloned.1.call-done, bf16[3696,8192]{1,0:T(8,128)(2,1)} %param.17), kind=kOutput, calls=%fused_computation.62 | convolution fusion | flops 7751073792 | bytes 64544768 | tf_op jit(solution)/shard_map/dot_general | solution.py:90
  249.6 1.7 multiply_convert_fusion
  253.3 18.1 %psum.23 = f32[4,32,32]{2,1,0:T(8,128)S(1)} all-reduce(f32[4,32,32]{2,1,0:T(8,128)} %fusion.37), channel_id=1, replica_groups=mesh['groups'=2,'tenant'=4,'tensor'=4] {'tensor'}, use_global_device_ids=true, to_apply=%region_9.10 | all-reduce | flops 4096 | bytes 32768 | tf_op jit(solution)/shard_map/psum | solution.py:102
  271.5 4.4 %fusion = f32[4,32,3696]{2,1,0:T(8,128)} fusion(bf16[4,32,3696]{2,1,0:T(8,128)(2,1)} %copy-done.3, f32[4,32,3696]{2,1,0:T(8,128)} %param.23, f32[4,32,3696]{2,1,0:T(8,128)S(1)} %copy-done.5, f32[4,32,32]{2,1,0:T(8,128)S(1)} %get-tuple-element.4), kind=kOutput, calls=%fused_computation.9 | convolution fusion | flops 183562240 | bytes 6639616 | tf_op jit(solution)/shard_map/bji,bjw->biw/dot_general | solution.py:106
  275.9 1.8 fusion.4
  (51 shorter events, 14.1 us)
Async XLA Ops:
  7.2 56.5 %copy-start = (bf16[4,32,3696]{2,1,0:T(8,128)(2,1)S(1)}, bf16[4,32,3696]{2,1,0:T(8,128)(2,1)}, u32[]{:S(2)}) copy-start(bf16[4,32,3696]{2,1,0:T(8,128)(2,1)} %param.19) | copy-start | bytes 2838532
  7.2 8.4 %copy-start.2 = (bf16[128,2048]{1,0:T(8,128)(2,1)S(1)}, bf16[128,2048]{1,0:T(8,128)(2,1)}, u32[]{:S(2)}) copy-start(bf16[128,2048]{1,0:T(8,128)(2,1)} %param.12) | copy-start | bytes 1572868
  11.3 7.9 %all-to-all-start = ((s32[4,32,1]{1,2,0:T(1,128)}), s32[4,32,1]{1,2,0:T(1,128)S(1)}, u32[]{:S(2)}, u32[]{:S(2)}) async-start(s32[4,32,1]{1,2,0:T(1,128)} %bitcast), calls=%async_computation | async-start | bytes 4096 | tf_op jit(solution)/shard_map/all_to_all | solution.py:57
  15.6 7.2 %copy-start.9 = (bf16[128,3696]{0,1:T(8,128)(2,1)S(1)}, bf16[128,3696]{0,1:T(8,128)(2,1)}, u32[]{:S(2)}) copy-start(bf16[128,3696]{0,1:T(8,128)(2,1)} %param.13) | copy-start | bytes 2838532
  19.2 12.3 %all-to-all-start.1 = ((bf16[4,32,2048]{2,1,0:T(8,128)(2,1)}), bf16[4,32,2048]{2,1,0:T(8,128)(2,1)S(1)}, u32[]{:S(2)}, u32[]{:S(2)}) async-start(bf16[4,32,2048]{2,1,0:T(8,128)(2,1)} %bitcast.2), calls=%async_computation.1 | async-start | bytes 1048576 | tf_op jit(solution)/shard_map/all_to_all | solution.py:49
  26.0 13.9 %copy-start.6 = (f32[4,2048,32]{1,2,0:T(8,128)S(1)}, f32[4,2048,32]{1,2,0:T(8,128)}, u32[]{:S(2)}) copy-start(f32[4,2048,32]{1,2,0:T(8,128)} %param.20) | copy-start | bytes 3145732
  31.5 0.8 copy-start.10
  32.3 33.5 %all-to-all-start.2 = ((bf16[4,32,3696]{2,1,0:T(8,128)(2,1)}), bf16[4,32,3696]{2,1,0:T(8,128)(2,1)S(1)}, u32[]{:S(2)}, u32[]{:S(2)}) async-start(bf16[4,32,3696]{2,1,0:T(8,128)(2,1)} %bitcast.5), calls=%async_computation.2 | async-start | bytes 1900544 | tf_op jit(solution)/shard_map/all_to_all | solution.py:50
  35.8 137.2 %reduce-scatter.2.cloned.1.call-start = ((), (), s32[]{:S(2)}) async-start(), calls=%async_computation.5 | async-start | bytes 5242880 | tf_op jit(solution)/shard_map/reduce_scatter | solution.py:88
  68.7 1.8 copy-start.4
  97.5 0.7 copy-start.1
  97.6 124.2 %all-gather.2.cloned.1.call-start = ((), (), s32[]{:S(2)}) async-start(), calls=%async_computation.6 | async-start | bytes 2621440 | tf_op jit(solution)/shard_map/all_gather | solution.py:91
  251.3 0.9 copy-start.3
  252.3 19.2 %copy-start.5 = (f32[4,32,3696]{2,1,0:T(8,128)S(1)}, f32[4,32,3696]{2,1,0:T(8,128)}, u32[]{:S(2)}) copy-start(f32[4,32,3696]{2,1,0:T(8,128)} %param.21) | copy-start | bytes 5677060
  271.5 4.4 %copy-start.7 = (f32[4,2048,32]{1,2,0:T(8,128)S(1)}, f32[4,2048,32]{1,2,0:T(8,128)}, u32[]{:S(2)}) copy-start(f32[4,2048,32]{1,2,0:T(8,128)} %param.20) | copy-start | bytes 3145732
  271.5 4.4 %copy-start.8 = (f32[4,2048,32]{1,2,0:T(8,128)S(1)}, f32[4,2048,32]{1,2,0:T(8,128)}, u32[]{:S(2)}) copy-start(f32[4,2048,32]{1,2,0:T(8,128)} %param.22) | copy-start | bytes 3145732
Sparse Core Ops, SparseCore 0:
  97.7 75.2 reduce-scatter.1
  175.3 46.4 all-gather.1
where the time goes:
time: 285 us; the launch traced here: 284 us
  waiting for transfers between devices  118 us (41%)
  matrix products  67.4 us (24%)
  blocking collectives  47.1 us (17%)
  local copies, waits for them, and re-layouts  18.4 us (6%)
  between operations  14.3 us (5%)
  starting transfers between devices  11.3 us (4%)
  other arithmetic  7.59 us (3%)
    reduce_scatter x1, waiting for transfers between devices, shards(): lax.psum_scatter(out_tan, 'tensor', scatter_dimension=1, tiled=True)  65.5 us
    all_gather x1, waiting for transfers between devices, shards(): lax.all_gather(row_cot, 'tensor', axis=1, tiled=True)  46.6 us
    dot_general x1, matrix products, shards(): lax.dot_general(lax.all_gather(row_cot, 'tensor', axis=1, tiled=True), do...  27.9 us
    dot_general x1, matrix products, shards(): jnp.dot(hidden_tan, down_projection_weight, preferred_element_type=jnp.fl...  23.6 us
    psum x1, blocking collectives, shards(): summed_p, summed_q = lax.psum((partial_product, part_q), 'tensor')  22.5 us
    psum x1, blocking collectives, shards(): lax.psum(partial_backward, 'tensor') / math.sqrt(ADAPTER_RANK)  18.1 us
    all_to_all x1, blocking collectives, shards(): lax.all_to_all(row_loss_curvature[send_order], 'tenant', split_axis=0, co...  6.47 us
  transfers between devices with their start and end apart: 5, of which 4 were waited for; matrix products, arithmetic and copies ran while one was open for 6% of the time, Pallas kernels for 0%

commit v1 on v0

--- a/solution.py
+++ b/solution.py
@@ -1,8 +1,11 @@
+import functools
 import math
 
 import jax
 import jax.numpy as jnp
 from jax import lax
+from jax.experimental import pallas as pl
+from jax.experimental.pallas import tpu as pltpu
 from jax.sharding import PartitionSpec as P
 
 MODEL_WIDTH = 8192
@@ -11,6 +14,239 @@
 
 damping = 0.05
 lissa_scale = 2.0
+
+
+LINE = 4
+COLS = 256
+MESH = pl.DeviceIdType.MESH
+
+
+def line_kernel(
+    nb, resident, streams,
+    h_ref, w_ref, gate_ref, weight_ref, cot_ref, e_ref,
+    wbuf, y, from_left, from_right, outgoing, cot, acc,
+    wsem, left_sem, right_sem, sum_send, cot_sem, cot_send_right, cot_send_left,
+):
+    n = LINE
+    me = lax.axis_index("tensor")
+    share = nb * COLS
+    hidden = h_ref.shape[1]
+    streamed = nb - resident
+
+    def fetch(slot, b, q):
+        cols = pl.ds(pl.multiple_of(q * share + b * COLS, COLS), COLS)
+        return pltpu.make_async_copy(
+            weight_ref.at[:, cols], wbuf.at[slot, :, pl.ds(q * COLS, COLS)], wsem.at[slot, q]
+        )
+
+    def sum_copy(b, q, to_right):
+        return pltpu.make_async_remote_copy(
+            src_ref=outgoing.at[b, q],
+            dst_ref=(from_left if to_right else from_right).at[b, q],
+            send_sem=sum_send.at[b, q],
+            recv_sem=(left_sem if to_right else right_sem).at[b, q],
+            device_id={"tensor": me + 1 if to_right else me - 1},
+            device_id_type=MESH,
+        )
+
+    def cot_copy(b, o, to_right):
+        block = cot.at[b, :, pl.ds(o * COLS, COLS)]
+        return pltpu.make_async_remote_copy(
+            src_ref=block,
+            dst_ref=block,
+            send_sem=(cot_send_right if to_right else cot_send_left).at[b, o],
+            recv_sem=cot_sem.at[b, o],
+            device_id={"tensor": me + 1 if to_right else me - 1},
+            device_id_type=MESH,
+        )
+
+    for b in range(resident):
+        for q in range(n):
+            fetch(b, b, q).start()
+    for u in range(streams):
+        for q in range(n):
+            fetch(resident + u, resident + u, q).start()
+
+    barrier = pltpu.get_barrier_semaphore()
+    for neighbour in (lax.rem(me + 1, n), lax.rem(me + n - 1, n)):
+        pl.semaphore_signal(barrier, inc=1, device_id={"tensor": neighbour}, device_id_type=MESH)
+    pl.semaphore_wait(barrier, 2)
+
+    acc[...] = jnp.zeros_like(acc)
+
+    def advance_sums(i):
+        for q in range(n):
+            hops = jnp.where(
+                me < q, me, jnp.where(me > q, n - 1 - me, jnp.maximum(me, n - 1 - me))
+            )
+            b = i - 1 - hops
+
+            @pl.when((b >= 0) & (b < nb))
+            def _():
+                @pl.when((me <= q) & (me > 0))
+                def _():
+                    sum_copy(b, q, True).wait_recv()
+                    y[b, q] += from_left[b, q].astype(jnp.float32)
+
+                @pl.when((me >= q) & (me < n - 1))
+                def _():
+                    sum_copy(b, q, False).wait_recv()
+                    y[b, q] += from_right[b, q].astype(jnp.float32)
+
+                @pl.when(me < q)
+                def _():
+                    outgoing[b, q] = y[b, q].astype(jnp.bfloat16)
+                    sum_copy(b, q, True).start()
+
+                @pl.when(me > q)
+                def _():
+                    outgoing[b, q] = y[b, q].astype(jnp.bfloat16)
+                    sum_copy(b, q, False).start()
+
+                @pl.when(me == q)
+                def _():
+                    block = (w_ref[...] * y[b, q]).astype(jnp.bfloat16)
+                    cot[b, :, q * COLS : (q + 1) * COLS] = block
+                    cot_ref[:, pl.ds(pl.multiple_of(b * COLS, COLS), COLS)] = block
+
+                    @pl.when(me < n - 1)
+                    def _():
+                        cot_copy(b, q, True).start()
+
+                    @pl.when(me > 0)
+                    def _():
+                        cot_copy(b, q, False).start()
+
+    def advance_cots(i):
+        for o in range(n):
+            b = i - 1 - max(o, n - 1 - o) - jnp.abs(me - o)
+
+            @pl.when((b >= 0) & (b < nb) & (me != o))
+            def _():
+                cot_copy(b, o, True).wait_recv()
+
+                @pl.when((me > o) & (me < n - 1))
+                def _():
+                    cot_copy(b, o, True).start()
+
+                @pl.when((me < o) & (me > 0))
+                def _():
+                    cot_copy(b, o, False).start()
+
+    def refill(u):
+        later = u + streams
+
+        @pl.when((u >= 0) & (later < 2 * streamed))
+        def _():
+            for q in range(n):
+                fetch(resident + later % streams, resident + later % streamed, q).start()
+
+    last_lag = 2 * n - 1
+
+    def step(i, carry):
+        advance_sums(i)
+        advance_cots(i)
+
+        @pl.when(i < nb)
+        def _():
+            u = i - resident
+            slot = jnp.where(u < 0, i, resident + jnp.maximum(u, 0) % streams)
+            for q in range(n):
+                fetch(slot, i, q).wait()
+                y[i, q] = jnp.dot(
+                    h_ref[...],
+                    wbuf[slot, :, q * COLS : (q + 1) * COLS],
+                    preferred_element_type=jnp.float32,
+                )
+            refill(u)
+
+        @pl.when(i >= last_lag)
+        def _():
+            b = i - last_lag
+            u = b - resident
+            slot = jnp.where(u < 0, b, resident + (jnp.maximum(u, 0) + streamed) % streams)
+
+            @pl.when(u >= 0)
+            def _():
+                for q in range(n):
+                    fetch(slot, b, q).wait()
+
+            for start in range(0, hidden, 512):
+                size = min(512, hidden - start)
+                acc[:, start : start + size] += lax.dot_general(
+                    cot[b],
+                    wbuf[slot, start : start + size, :],
+                    (((1,), (1,)), ((), ())),
+                    preferred_element_type=jnp.float32,
+                )
+
+            @pl.when(u >= 0)
+            def _():
+                refill(u + streamed)
+
+        return carry
+
+    lax.fori_loop(0, nb + last_lag, step, 0)
+
+    for start in range(0, hidden, 512):
+        size = min(512, hidden - start)
+        gate = gate_ref[:, start : start + size].astype(jnp.float32)
+        e_ref[:, start : start + size] = (
+            gate / (1.0 + jnp.exp(-gate)) * acc[:, start : start + size]
+        ).astype(jnp.bfloat16)
+
+    def drain(b, carry):
+        for q in range(n):
+            @pl.when(me != q)
+            def _():
+                sum_copy(b, q, True).wait_send()
+
+            @pl.when((q <= me) & (me < n - 1))
+            def _():
+                cot_copy(b, q, True).wait_send()
+
+            @pl.when((q >= me) & (me > 0))
+            def _():
+                cot_copy(b, q, False).wait_send()
+
+        return carry
+
+    lax.fori_loop(0, nb, drain, 0)
+
+
+def line_products(hidden_tan, weights, gate, weight):
+    rows, hidden = hidden_tan.shape
+    width = weight.shape[1]
+    nb = width // (LINE * COLS)
+    resident, streams = 3, 2
+    bf16, f32 = jnp.bfloat16, jnp.float32
+    vmem = pl.BlockSpec(memory_space=pltpu.VMEM)
+    sems = pltpu.SemaphoreType.DMA
+    return pl.pallas_call(
+        functools.partial(line_kernel, nb, resident, streams),
+        out_shape=(
+            jax.ShapeDtypeStruct((rows, width // LINE), bf16),
+            jax.ShapeDtypeStruct((rows, hidden), bf16),
+        ),
+        in_specs=[vmem, vmem, vmem, pl.BlockSpec(memory_space=pl.ANY)],
+        out_specs=(vmem, vmem),
+        scratch_shapes=[
+            pltpu.VMEM((resident + streams, hidden, LINE * COLS), bf16),
+            pltpu.VMEM((nb, LINE, rows, COLS), f32),
+            pltpu.VMEM((nb, LINE, rows, COLS), bf16),
+            pltpu.VMEM((nb, LINE, rows, COLS), bf16),
+            pltpu.VMEM((nb, LINE, rows, COLS), bf16),
+            pltpu.VMEM((nb, rows, LINE * COLS), bf16),
+            pltpu.VMEM((rows, hidden), f32),
+            sems((resident + streams, LINE)),
+        ] + [sems((nb, LINE))] * 6,
+        compiler_params=pltpu.CompilerParams(
+            collective_id=0, has_side_effects=True, vmem_limit_bytes=60 * 1024 * 1024
+        ),
+        cost_estimate=pl.CostEstimate(
+            flops=4 * rows * hidden * width, bytes_accessed=3 * hidden * width, transcendentals=0
+        ),
+    )(hidden_tan, weights, gate, weight)
 
 
 def shards(
@@ -84,18 +320,29 @@
         local_tenant_count, rows_each, f_local
     )
     hidden_tan = (gate_act * up_tangent).astype(jnp.bfloat16).reshape(row_count, f_local)
-    out_tan = jnp.dot(hidden_tan, down_projection_weight, preferred_element_type=jnp.float32)
-    out_share = lax.psum_scatter(out_tan, "tensor", scatter_dimension=1, tiled=True)
-    row_cot = (weights[:, None] * out_share).astype(jnp.bfloat16)
-    hidden_bar = lax.dot_general(
-        lax.all_gather(row_cot, "tensor", axis=1, tiled=True),
-        down_projection_weight,
-        (((1,), (1,)), ((), ())),
-        preferred_element_type=jnp.float32,
-    )
-    up_cotangent = (gate_act * hidden_bar.reshape(local_tenant_count, rows_each, f_local)).astype(
-        jnp.bfloat16
-    )
+    if (
+        lax.axis_size("tensor") == LINE
+        and row_count % 16 == 0
+        and f_local % 16 == 0
+        and down_projection_weight.shape[1] % (LINE * COLS) == 0
+    ):
+        row_cot, up_cotangent = line_products(
+            hidden_tan, weights[:, None], grouped_gate, down_projection_weight
+        )
+        up_cotangent = up_cotangent.reshape(local_tenant_count, rows_each, f_local)
+    else:
+        out_tan = jnp.dot(hidden_tan, down_projection_weight, preferred_element_type=jnp.float32)
+        out_share = lax.psum_scatter(out_tan, "tensor", scatter_dimension=1, tiled=True)
+        row_cot = (weights[:, None] * out_share).astype(jnp.bfloat16)
+        hidden_bar = lax.dot_general(
+            lax.all_gather(row_cot, "tensor", axis=1, tiled=True),
+            down_projection_weight,
+            (((1,), (1,)), ((), ())),
+            preferred_element_type=jnp.float32,
+        )
+        up_cotangent = (gate_act * hidden_bar.reshape(local_tenant_count, rows_each, f_local)).astype(
+            jnp.bfloat16
+        )
     partial_backward = jnp.einsum(
         "acv,apv->acp", up_cotangent, adapter_output_factors, preferred_element_type=jnp.float32
     )

time: 285 us -> 183 us (0.64)
  waiting for transfers between devices: 118 us -> 7.22 us
  Pallas kernels: 0 us -> 75.4 us
  matrix products: 67.4 us -> 19.6 us
  between operations: 14.3 us -> 0.88 us
  blocking collectives: 47.1 us -> 41.5 us
  other arithmetic: 7.59 us -> 2.43 us
  starting transfers between devices: 11.3 us -> 14.4 us
    pallas_call x0 -> x1, Pallas kernels: none -> 75.4 us  [line_products(): pl.pallas_call(functools.partial(line_kernel, nb, resident, streams), out...]
    reduce_scatter x1 -> x0, waiting for transfers between devices: 65.5 us -> none  [shards(): lax.psum_scatter(out_tan, 'tensor', scatter_dimension=1, tiled=True)]
    dot_general x2 -> x0, matrix products: 51.5 us -> none  [the longest x1 27.9 us: shards(): lax.dot_general(lax.all_gather(row_cot, 'tensor', axis=1, tiled=True), do...]
    all_gather x1 -> x0, waiting for transfers between devices: 46.6 us -> none  [shards(): lax.all_gather(row_cot, 'tensor', axis=1, tiled=True)]
    all_to_all x1 -> x0, blocking collectives: 6.47 us -> none  [shards(): lax.all_to_all(row_loss_curvature[send_order], 'tenant', split_axis=0, co...]
    all_to_all x0 -> x1, starting transfers between devices: none -> 4.21 us  [shards(): lax.all_to_all(row_loss_curvature[send_order], 'tenant', split_axis=0, co...]
    convert_element_type x3 -> x0, other arithmetic: 3.84 us -> none  [the longest x1 2.14 us: shards(): row_cot = (weights[:, None] * out_share).astype(jnp.bfloat16)]
  transfers between devices with their start and end apart: 5 -> 4, of which waited for: 4 -> 2; matrix products, arithmetic and copies ran while one was open for 6% -> 10% of each run, Pallas kernels for 0% -> 0%
where the time goes in v1:
time: 183 us
  Pallas kernels  75.4 us (41%)
  blocking collectives  41.5 us (23%)
  local copies, waits for them, and re-layouts  21 us (11%)
  matrix products  19.6 us (11%)
  starting transfers between devices  14.4 us (8%)
  waiting for transfers between devices  7.22 us (4%)
  other arithmetic  2.43 us (1%)
    pallas_call x1, Pallas kernels, line_products(): pl.pallas_call(functools.partial(line_kernel, nb, resident, streams), out...  75.4 us
    psum x1, blocking collectives, shards(): summed_p, summed_q = lax.psum((partial_product, part_q), 'tensor')  23 us
    psum x1, blocking collectives, shards(): lax.psum(partial_backward, 'tensor') / math.sqrt(ADAPTER_RANK)  18.5 us
    all_to_all x1, waiting for transfers between devices, shards(): lax.all_to_all(feats[send_order], 'tenant', split_axis=0, concat_axis=0,...  5.43 us
    dot_general x1, matrix products, shards(): jnp.einsum('wqh,whx->wqx', project_rows, iterate_output_factors, precisio...  4.38 us
    unnamed x22, local copies, waits for them, and re-layouts  4.35 us
    dot_general x1, matrix products, shards(): jnp.einsum('bji,bjw->biw', project_rows, up_cotangent.astype(jnp.float32)...  4.34 us
    all_to_all x1, starting transfers between devices, shards(): lax.all_to_all(row_loss_curvature[send_order], 'tenant', split_axis=0, co...  4.21 us
  transfers between devices with their start and end apart: 4, of which 2 were waited for; matrix products, arithmetic and copies ran while one was open for 10% of the time, Pallas kernels for 0%

profile of v1, /device:TPU:0, one launch (start us, length us, event | category | flops | bytes accessed | tf_op | source)
XLA Modules:
  0.0 182.5 jit_solution(9850336458508141346)
XLA Ops:
  2.9 1.6 gather_fusion.3
  5.2 4.2 %all-to-all-start.3 = ((bf16[4,32,1]{1,2,0:T(2,128)(2,1)}), bf16[4,32,1]{1,2,0:T(2,128)(2,1)S(1)}, u32[]{:S(2)}, u32[]{:S(2)}) async-start(bf16[4,32,1]{1,2,0:T(2,128)(2,1)} %all_to_all.44), calls=%async_computation.3 | async-start | bytes 4096 | tf_op jit(solution)/shard_map/all_to_all | solution.py:289
  9.4 1.2 gather_fusion
  11.3 1.8 all-to-all-done.3
  13.1 3.2 %all-to-all-start = ((s32[4,32,1]{1,2,0:T(1,128)}), s32[4,32,1]{1,2,0:T(1,128)S(1)}, u32[]{:S(2)}, u32[]{:S(2)}) async-start(s32[4,32,1]{1,2,0:T(1,128)} %bitcast), calls=%async_computation | async-start | bytes 4096 | tf_op jit(solution)/shard_map/all_to_all | solution.py:293
  16.3 1.7 gather_fusion.1
  19.2 2.1 %gather_fusion.2 = bf16[128,3696]{1,0:T(8,128)(2,1)} fusion(bf16[128,3696]{1,0:T(8,128)(2,1)S(1)} %copy.28, s32[1024]{0:T(1024)S(1)} %pad_clamp_fusion), kind=kCustom, calls=%fused_computation.2 | custom fusion | bytes 1892864 | tf_op jit(solution)/shard_map/gather | solution.py:287
  21.4 3.5 %all-to-all-start.1 = ((bf16[4,32,2048]{2,1,0:T(8,128)(2,1)}), bf16[4,32,2048]{2,1,0:T(8,128)(2,1)S(1)}, u32[]{:S(2)}, u32[]{:S(2)}) async-start(bf16[4,32,2048]{2,1,0:T(8,128)(2,1)} %bitcast.2), calls=%async_computation.1 | async-start | bytes 1048576 | tf_op jit(solution)/shard_map/all_to_all | solution.py:285
  26.2 1.3 scatter_custom_fusion.3
  28.3 5.4 %all-to-all-done.1 = bf16[4,32,2048]{2,1,0:T(8,128)(2,1)S(1)} async-done(((bf16[4,32,2048]{2,1,0:T(8,128)(2,1)}), bf16[4,32,2048]{2,1,0:T(8,128)(2,1)S(1)}, u32[]{:S(2)}, u32[]{:S(2)}) %all-to-all-start.1) | async-done | bytes 524320 | tf_op jit(solution)/shard_map/all_to_all | solution.py:285
  33.7 3.5 %all-to-all-start.2 = ((bf16[4,32,3696]{2,1,0:T(8,128)(2,1)}), bf16[4,32,3696]{2,1,0:T(8,128)(2,1)S(1)}, u32[]{:S(2)}, u32[]{:S(2)}) async-start(bf16[4,32,3696]{2,1,0:T(8,128)(2,1)} %bitcast.5), calls=%async_computation.2 | async-start | bytes 1900544 | tf_op jit(solution)/shard_map/all_to_all | solution.py:286
  37.2 2.0 %scatter_custom_fusion.1 = bf16[128,2048]{1,0:T(8,128)(2,1)S(1)} fusion(s32[128]{0:T(128)S(1)} %fusion.24, bf16[128,2048]{1,0:T(8,128)(2,1)} %bitcast.33, bf16[]{:T(256)} %constant.56.clone.1), kind=kCustom, calls=%fused_computation.23 | custom fusion | bytes 524800 | tf_op jit(solution)/shard_map/scatter | solution.py:296
  39.2 2.0 %fusion.34 = f32[4,32,32]{2,1,0:T(8,128)} fusion(bf16[4,32,2048]{2,1,0:T(8,128)(2,1)S(1)} %bitcast.25, bf16[4,2048,32]{1,2,0:T(8,128)(2,1)} %param.18), kind=kOutput, calls=%fused_computation.59 | convolution fusion | flops 16777216 | bytes 1064960 | tf_op jit(solution)/shard_map/ake,aex->akx/dot_general | solution.py:301
  41.2 1.3 fusion.33
  42.5 23.0 %all-reduce = (f32[4,32,32]{2,1,0:T(8,128)}, f32[4,32,32]{2,1,0:T(8,128)S(1)}) all-reduce(f32[4,32,32]{2,1,0:T(8,128)} %fusion.33, f32[4,32,32]{2,1,0:T(8,128)} %fusion.34), channel_id=1, replica_groups=mesh['groups'=2,'tenant'=4,'tensor'=4] {'tensor'}, use_global_device_ids=true, to_apply=%region_5.6 | all-reduce | flops 8192 | bytes 65536 | tf_op jit(solution)/shard_map/psum | solution.py:305
  65.5 3.0 %fusion.13 = f32[4,32,3696]{2,1,0:T(8,128)} fusion(bf16[4,32,3696]{2,1,0:T(8,128)(2,1)S(1)} %copy-done, f32[4,32,32]{2,1,0:T(8,128)} %get-tuple-element.7), kind=kOutput, calls=%fused_computation.26 | convolution fusion | flops 181669888 | bytes 2854912 | tf_op jit(solution)/shard_map/wqh,whx->wqx/dot_general | solution.py:309
  69.4 3.0 %scatter_custom_fusion.2.gate_ref = bf16[128,3696]{1,0:T(8,128)(2,1)S(1)} fusion(s32[128]{0:T(128)S(1)} %fusion.24, bf16[128,3696]{1,0:T(8,128)(2,1)} %bitcast.32, bf16[]{:T(256)} %constant.56.clone.1), kind=kCustom, calls=%fused_computation.21 | custom fusion | bytes 946688 | tf_op jit(solution)/shard_map/scatter | solution.py:297
  72.9 1.3 copy-done.3
  74.3 4.4 %fusion.3 = bf16[4,32,3696]{2,1,0:T(8,128)(2,1)} fusion(f32[4,32,3696]{2,1,0:T(8,128)S(1)} %bitcast.28, f32[4,32,3696]{2,1,0:T(8,128)} %fusion.13, f32[4,32,3696]{2,1,0:T(8,128)S(1)} %copy-done.3, f32[4,32,32]{2,1,0:T(8,128)S(1)} %get-tuple-element.8), kind=kOutput, calls=%fused_computation.13 | convolution fusion | flops 183562240 | bytes 6639616 | tf_op jit(solution)/shard_map/wqh,whx->wqx/dot_general | solution.py:315
  78.7 75.4 %shard_map.139 = (bf16[128,2048]{1,0:T(8,128)(2,1)}, bf16[128,3696]{1,0:T(8,128)(2,1)}) custom-call(bf16[128,3696]{1,0:T(8,128)(2,1)} %bitcast.31, f32[128,1]{1,0:T(8,128)} %copy.30.w_ref, bf16[128,3696]{1,0:T(8,128)(2,1)} %copy-done.2, bf16[3696,8192]{1,0:T(8,128)(2,1)} %weight_ref.1), custom_call_target="tpu_custom_call" | custom-call | flops 15502147584 | bytes 90832896 | tf_op jit(solution)/shard_map/pallas_call | solution.py:225
  154.1 1.7 fusion.35
  155.9 4.3 %fusion = f32[4,32,3696]{2,1,0:T(8,128)} fusion(bf16[4,32,3696]{2,1,0:T(8,128)(2,1)} %bitcast.30, f32[4,32,3696]{2,1,0:T(8,128)} %param.23, f32[4,32,3696]{2,1,0:T(8,128)S(1)} %copy-done.4, f32[4,32,32]{2,1,0:T(8,128)S(1)} %get-tuple-element.8), kind=kOutput, calls=%fused_computation.9 | convolution fusion | flops 183562240 | bytes 6639616 | tf_op jit(solution)/shard_map/bji,bjw->biw/dot_general | solution.py:353
  160.3 18.5 %psum.23 = f32[4,32,32]{2,1,0:T(8,128)S(1)} all-reduce(f32[4,32,32]{2,1,0:T(8,128)S(1)} %fusion.35), channel_id=1, replica_groups=mesh['groups'=2,'tenant'=4,'tensor'=4] {'tensor'}, use_global_device_ids=true, to_apply=%region_8.9 | all-reduce | flops 4096 | bytes 32768 | tf_op jit(solution)/shard_map/psum | solution.py:349
  178.7 3.0 %fusion.4 = f32[4,2048,32]{1,2,0:T(8,128)} fusion(bf16[4,32,2048]{2,1,0:T(8,128)(2,1)S(1)} %bitcast.27, f32[4,2048,32]{1,2,0:T(8,128)} %param.22, f32[4,2048,32]{1,2,0:T(8,128)S(1)} %copy-done.5, f32[4,32,32]{2,1,0:T(8,128)S(1)} %psum.23), kind=kOutput, calls=%fused_computation.15 | convolution fusion | flops 101715968 | bytes 3686400 | tf_op jit(solution)/shard_map/tsd,tsr->tdr/dot_general | solution.py:350
  (43 shorter events, 9.2 us)
Async XLA Ops:
  0.6 64.9 %copy-start = (bf16[4,32,3696]{2,1,0:T(8,128)(2,1)S(1)}, bf16[4,32,3696]{2,1,0:T(8,128)(2,1)}, u32[]{:S(2)}) copy-start(bf16[4,32,3696]{2,1,0:T(8,128)(2,1)} %param.19) | copy-start | bytes 2838532
  0.6 15.7 %copy-start.1 = (bf16[128,2048]{1,0:T(8,128)(2,1)S(1)}, bf16[128,2048]{1,0:T(8,128)(2,1)}, u32[]{:S(2)}) copy-start(bf16[128,2048]{1,0:T(8,128)(2,1)} %param.12) | copy-start | bytes 1572868
  5.2 7.9 %all-to-all-start.3 = ((bf16[4,32,1]{1,2,0:T(2,128)(2,1)}), bf16[4,32,1]{1,2,0:T(2,128)(2,1)S(1)}, u32[]{:S(2)}, u32[]{:S(2)}) async-start(bf16[4,32,1]{1,2,0:T(2,128)(2,1)} %all_to_all.44), calls=%async_computation.3 | async-start | bytes 4096 | tf_op jit(solution)/shard_map/all_to_all | solution.py:289
  13.1 8.3 %all-to-all-start = ((s32[4,32,1]{1,2,0:T(1,128)}), s32[4,32,1]{1,2,0:T(1,128)S(1)}, u32[]{:S(2)}, u32[]{:S(2)}) async-start(s32[4,32,1]{1,2,0:T(1,128)} %bitcast), calls=%async_computation | async-start | bytes 4096 | tf_op jit(solution)/shard_map/all_to_all | solution.py:293
  16.3 1.7 copy-start.7
  21.4 12.3 %all-to-all-start.1 = ((bf16[4,32,2048]{2,1,0:T(8,128)(2,1)}), bf16[4,32,2048]{2,1,0:T(8,128)(2,1)S(1)}, u32[]{:S(2)}, u32[]{:S(2)}) async-start(bf16[4,32,2048]{2,1,0:T(8,128)(2,1)} %bitcast.2), calls=%async_computation.1 | async-start | bytes 1048576 | tf_op jit(solution)/shard_map/all_to_all | solution.py:285
  24.9 16.3 %copy-start.5 = (f32[4,2048,32]{1,2,0:T(8,128)S(1)}, f32[4,2048,32]{1,2,0:T(8,128)}, u32[]{:S(2)}) copy-start(f32[4,2048,32]{1,2,0:T(8,128)} %param.20) | copy-start | bytes 3145732
  33.7 3.5 %copy-start.8 = (bf16[4,32,2048]{2,1,0:T(8,128)(2,1)}, bf16[4,32,2048]{2,1,0:T(8,128)(2,1)S(1)}, u32[]{:S(2)}) copy-start(bf16[4,32,2048]{2,1,0:T(8,128)(2,1)S(1)} %all-to-all-done.1) | copy-start | bytes 1572868
  33.7 34.8 %all-to-all-start.2 = ((bf16[4,32,3696]{2,1,0:T(8,128)(2,1)}), bf16[4,32,3696]{2,1,0:T(8,128)(2,1)S(1)}, u32[]{:S(2)}, u32[]{:S(2)}) async-start(bf16[4,32,3696]{2,1,0:T(8,128)(2,1)} %bitcast.5), calls=%async_computation.2 | async-start | bytes 1900544 | tf_op jit(solution)/shard_map/all_to_all | solution.py:286
  68.5 0.9 copy-start.6
  72.4 6.3 %copy-start.2 = (bf16[128,3696]{1,0:T(8,128)(2,1)}, bf16[128,3696]{1,0:T(8,128)(2,1)S(1)}, u32[]{:S(2)}) copy-start(bf16[128,3696]{1,0:T(8,128)(2,1)S(1)} %scatter_custom_fusion.2.gate_ref) | copy-start | bytes 2838532
  72.4 1.9 %copy-start.3 = (f32[4,32,3696]{2,1,0:T(8,128)S(1)}, f32[4,32,3696]{2,1,0:T(8,128)}, u32[]{:S(2)}) copy-start(f32[4,32,3696]{2,1,0:T(8,128)} %param.21) | copy-start | bytes 5677060
  154.1 1.8 copy-start.4
  178.7 3.0 %copy-start.9 = (bf16[128,2048]{1,0:T(8,128)(2,1)S(1)}, bf16[128,2048]{1,0:T(8,128)(2,1)}, u32[]{:S(2)}) copy-start(bf16[128,2048]{1,0:T(8,128)(2,1)} %get-tuple-element.16) | copy-start | bytes 1572868

commit v2 on v1

--- a/solution.py
+++ b/solution.py
@@ -247,6 +247,178 @@
             flops=4 * rows * hidden * width, bytes_accessed=3 * hidden * width, transcendentals=0
         ),
     )(hidden_tan, weights, gate, weight)
+
+
+def greet(axis, n):
+    me = lax.axis_index(axis)
+    barrier = pltpu.get_barrier_semaphore()
+    for k in range(1, n):
+        pl.semaphore_signal(
+            barrier, inc=1, device_id={axis: lax.rem(me + k, n)}, device_id_type=MESH
+        )
+    pl.semaphore_wait(barrier, n - 1)
+    return me
+
+
+def sum_kernel(x_ref, out_ref, got, send_sem, recv_sem):
+    me = greet("tensor", LINE)
+    copies = [
+        pltpu.make_async_remote_copy(
+            src_ref=x_ref,
+            dst_ref=got.at[k - 1],
+            send_sem=send_sem.at[k - 1],
+            recv_sem=recv_sem.at[k - 1],
+            device_id={"tensor": lax.rem(me + k, LINE)},
+            device_id_type=MESH,
+        )
+        for k in range(1, LINE)
+    ]
+    for copy in copies:
+        copy.start()
+    for copy in copies:
+        copy.wait_recv()
+    out_ref[...] = x_ref[...] + got[0] + got[1] + got[2]
+    for copy in copies:
+        copy.wait_send()
+
+
+def tensor_sum(x, collective_id):
+    vmem = pl.BlockSpec(memory_space=pltpu.VMEM)
+    return pl.pallas_call(
+        sum_kernel,
+        out_shape=jax.ShapeDtypeStruct(x.shape, x.dtype),
+        in_specs=[vmem],
+        out_specs=vmem,
+        scratch_shapes=[
+            pltpu.VMEM((LINE - 1,) + x.shape, x.dtype),
+            pltpu.SemaphoreType.DMA((LINE - 1,)),
+            pltpu.SemaphoreType.DMA((LINE - 1,)),
+        ],
+        compiler_params=pltpu.CompilerParams(
+            collective_id=collective_id,
+            has_side_effects=True,
+            vmem_limit_bytes=16 * 1024 * 1024,
+        ),
+    )(x)
+
+
+def exchange_kernel(
+    n, x_ref, gate_ref, meta_ref, x_out, gate_out, w_out,
+    x_send, gate_send, meta_send, x_got, gate_got, meta_got, send_sem, recv_sem,
+):
+    bf16, f32 = jnp.bfloat16, jnp.float32
+    rows = x_ref.shape[0]
+    per = rows // n
+    me = lax.axis_index("tenant")
+
+    def moved(select, source):
+        return lax.dot_general(
+            select, source, (((0,), (0,)), ((), ())), preferred_element_type=f32
+        )
+
+    lane = lax.broadcasted_iota(jnp.int32, (rows, rows), 1)
+    earlier = (lane < lax.broadcasted_iota(jnp.int32, (rows, rows), 0)).astype(f32).astype(bf16)
+    lane = lane.astype(f32)
+    meta = meta_ref[...]
+    target = meta[:, 1:2]
+    matches = (target == lane).astype(f32)
+    counts = jnp.dot(earlier, matches.astype(bf16), preferred_element_type=f32)
+    within = jnp.sum(counts * matches, axis=1, keepdims=True)
+    order = (target * per + within == lane).astype(f32).astype(bf16)
+
+    def spread(source_ref, send_ref):
+        width = source_ref.shape[1]
+        for start in range(0, width, 512):
+            size = min(512, width - start)
+            block = moved(order, source_ref[:, start : start + size].astype(bf16)).astype(bf16)
+            for t in range(n):
+                send_ref[t, :, start : start + size] = block[t * per : (t + 1) * per]
+
+    def copies(which, send_ref, got_ref):
+        return [
+            pltpu.make_async_remote_copy(
+                src_ref=send_ref.at[lax.rem(me + k, n)],
+                dst_ref=got_ref.at[k],
+                send_sem=send_sem.at[which, k],
+                recv_sem=recv_sem.at[which, k],
+                device_id={"tenant": lax.rem(me + k, n)},
+                device_id_type=MESH,
+            )
+            for k in range(1, n)
+        ]
+
+    spread(meta_ref, meta_send)
+    spread(x_ref, x_send)
+    greet("tenant", n)
+    meta_copies = copies(0, meta_send, meta_got)
+    x_copies = copies(1, x_send, x_got)
+    gate_copies = copies(2, gate_send, gate_got)
+    for copy in meta_copies + x_copies:
+        copy.start()
+    spread(gate_ref, gate_send)
+    for copy in gate_copies:
+        copy.start()
+    meta_got[0] = meta_send[me]
+    x_got[0] = x_send[me]
+    gate_got[0] = gate_send[me]
+
+    for copy in meta_copies:
+        copy.wait_recv()
+    meta_rows = meta_got[...].reshape(rows, meta_ref.shape[1])
+    place = (meta_rows[:, 2:3].astype(f32) == lane).astype(f32).astype(bf16)
+    w_out[...] = moved(place, meta_rows)[:, 0:1]
+
+    def settle(got_ref, out_ref):
+        width = out_ref.shape[1]
+        for start in range(0, width, 512):
+            size = min(512, width - start)
+            block = got_ref[:, :, start : start + size].reshape(rows, size)
+            out_ref[:, start : start + size] = moved(place, block).astype(bf16)
+
+    for copy in x_copies:
+        copy.wait_recv()
+    settle(x_got, x_out)
+    for copy in gate_copies:
+        copy.wait_recv()
+    settle(gate_got, gate_out)
+    for copy in meta_copies + x_copies + gate_copies:
+        copy.wait_send()
+
+
+def exchange(n, x, gate, weights, target, place):
+    rows = x.shape[0]
+    bf16, f32 = jnp.bfloat16, jnp.float32
+    column = jnp.arange(128)[None, :]
+    meta = jnp.where(
+        column == 0,
+        weights[:, None].astype(f32),
+        jnp.where(
+            column == 1,
+            target[:, None].astype(f32),
+            jnp.where(column == 2, place[:, None].astype(f32), 0.0),
+        ),
+    )
+    vmem = pl.BlockSpec(memory_space=pltpu.VMEM)
+    slots = [
+        pltpu.VMEM((n, rows // n, width), bf16) for width in (x.shape[1], gate.shape[1], 128)
+    ]
+    return pl.pallas_call(
+        functools.partial(exchange_kernel, n),
+        out_shape=(
+            jax.ShapeDtypeStruct(x.shape, bf16),
+            jax.ShapeDtypeStruct(gate.shape, bf16),
+            jax.ShapeDtypeStruct((rows, 1), f32),
+        ),
+        in_specs=[vmem] * 3,
+        out_specs=(vmem,) * 3,
+        scratch_shapes=slots + slots + [
+            pltpu.SemaphoreType.DMA((3, n)),
+            pltpu.SemaphoreType.DMA((3, n)),
+        ],
+        compiler_params=pltpu.CompilerParams(
+            collective_id=3, has_side_effects=True, vmem_limit_bytes=40 * 1024 * 1024
+        ),
+    )(x, gate, meta)
 
 
 def shards(
@@ -272,37 +444,57 @@
     d_local = feats.shape[1]
     f_local = gate_preactivation.shape[1]
     target = row_adapter_index // local_tenant_count
-    matches = (target[:, None] == jnp.arange(tenant_count, dtype=jnp.int32)[None, :]).astype(
-        jnp.int32
-    )
-    within = jnp.sum((jnp.cumsum(matches, axis=0) - 1) * matches, axis=1)
-    send_pos = target * per_dest + within
-    send_order = (
-        jnp.zeros((row_count,), jnp.int32).at[send_pos].set(jnp.arange(row_count, dtype=jnp.int32))
-    )
     place_local = row_adapter_index % local_tenant_count * rows_each + row_adapter_position
-    got_x, got_gate, got_weight = (
-        lax.all_to_all(feats[send_order], "tenant", split_axis=0, concat_axis=0, tiled=True),
-        lax.all_to_all(
-            gate_preactivation[send_order], "tenant", split_axis=0, concat_axis=0, tiled=True
-        ),
-        lax.all_to_all(
-            row_loss_curvature[send_order], "tenant", split_axis=0, concat_axis=0, tiled=True
-        ),
-    )
-    arrival = lax.all_to_all(
-        place_local[send_order], "tenant", split_axis=0, concat_axis=0, tiled=True
-    )
-    grouped_input_rows = jnp.zeros_like(got_x).at[arrival].set(got_x)
-    grouped_gate = jnp.zeros_like(got_gate).at[arrival].set(got_gate)
-    weights = jnp.zeros_like(got_weight).at[arrival].set(got_weight).astype(jnp.float32)
+    by_kernels = (
+        lax.axis_size("tensor") == LINE
+        and row_count == 128
+        and tenant_count > 1
+        and per_dest % 16 == 0
+        and f_local % 16 == 0
+        and down_projection_weight.shape[1] % (LINE * COLS) == 0
+    )
+    if by_kernels:
+        grouped_input_rows, grouped_gate, weights = exchange(
+            tenant_count, feats, gate_preactivation, row_loss_curvature, target, place_local
+        )
+    else:
+        matches = (target[:, None] == jnp.arange(tenant_count, dtype=jnp.int32)[None, :]).astype(
+            jnp.int32
+        )
+        within = jnp.sum((jnp.cumsum(matches, axis=0) - 1) * matches, axis=1)
+        send_pos = target * per_dest + within
+        send_order = (
+            jnp.zeros((row_count,), jnp.int32).at[send_pos].set(jnp.arange(row_count, dtype=jnp.int32))
+        )
+        got_x, got_gate, got_weight = (
+            lax.all_to_all(feats[send_order], "tenant", split_axis=0, concat_axis=0, tiled=True),
+            lax.all_to_all(
+                gate_preactivation[send_order], "tenant", split_axis=0, concat_axis=0, tiled=True
+            ),
+            lax.all_to_all(
+                row_loss_curvature[send_order], "tenant", split_axis=0, concat_axis=0, tiled=True
+            ),
+        )
+        arrival = lax.all_to_all(
+            place_local[send_order], "tenant", split_axis=0, concat_axis=0, tiled=True
+        )
+        grouped_input_rows = jnp.zeros_like(got_x).at[arrival].set(got_x)
+        grouped_gate = jnp.zeros_like(got_gate).at[arrival].set(got_gate)
+        weights = jnp.zeros_like(got_weight).at[arrival].set(got_weight).astype(jnp.float32)
+        weights = weights[:, None]
     input_three_axes = grouped_input_rows.reshape(local_tenant_count, rows_each, d_local)
     x_float = input_three_axes.astype(jnp.float32)
     partial_product = jnp.einsum(
         "ake,aex->akx", input_three_axes, adapter_input_factors, preferred_element_type=jnp.float32
     )
     part_q = jnp.einsum("ake,aex->akx", x_float, iterate_input_factors, precision=highest_precision)
-    summed_p, summed_q = lax.psum((partial_product, part_q), "tensor")
+    if by_kernels:
+        both = jnp.concatenate((partial_product, part_q), axis=2)
+        both = tensor_sum(both.reshape(row_count, 2 * ADAPTER_RANK), 1)
+        both = both.reshape(local_tenant_count, rows_each, 2 * ADAPTER_RANK)
+        summed_p, summed_q = both[:, :, :ADAPTER_RANK], both[:, :, ADAPTER_RANK:]
+    else:
+        summed_p, summed_q = lax.psum((partial_product, part_q), "tensor")
     project_rows = summed_p / math.sqrt(MODEL_WIDTH)
     lowrank_tangent = summed_q / math.sqrt(MODEL_WIDTH)
     up_tangent = (
@@ -320,20 +512,15 @@
         local_tenant_count, rows_each, f_local
     )
     hidden_tan = (gate_act * up_tangent).astype(jnp.bfloat16).reshape(row_count, f_local)
-    if (
-        lax.axis_size("tensor") == LINE
-        and row_count % 16 == 0
-        and f_local % 16 == 0
-        and down_projection_weight.shape[1] % (LINE * COLS) == 0
-    ):
+    if by_kernels:
         row_cot, up_cotangent = line_products(
-            hidden_tan, weights[:, None], grouped_gate, down_projection_weight
+            hidden_tan, weights, grouped_gate, down_projection_weight
         )
         up_cotangent = up_cotangent.reshape(local_tenant_count, rows_each, f_local)
     else:
         out_tan = jnp.dot(hidden_tan, down_projection_weight, preferred_element_type=jnp.float32)
         out_share = lax.psum_scatter(out_tan, "tensor", scatter_dimension=1, tiled=True)
-        row_cot = (weights[:, None] * out_share).astype(jnp.bfloat16)
+        row_cot = (weights * out_share).astype(jnp.bfloat16)
         hidden_bar = lax.dot_general(
             lax.all_gather(row_cot, "tensor", axis=1, tiled=True),
             down_projection_weight,
@@ -346,7 +533,13 @@
     partial_backward = jnp.einsum(
         "acv,apv->acp", up_cotangent, adapter_output_factors, preferred_element_type=jnp.float32
     )
-    lowrank_backward = lax.psum(partial_backward, "tensor") / math.sqrt(ADAPTER_RANK)
+    if by_kernels:
+        summed_backward = tensor_sum(
+            partial_backward.reshape(row_count, ADAPTER_RANK), 2
+        ).reshape(partial_backward.shape)
+    else:
+        summed_backward = lax.psum(partial_backward, "tensor")
+    lowrank_backward = summed_backward / math.sqrt(ADAPTER_RANK)
     curve_a = jnp.einsum(
         "tsd,tsr->tdr", x_float, lowrank_backward, precision=highest_precision
     ) / math.sqrt(MODEL_WIDTH)

time: 183 us -> 134 us (0.73)
  Pallas kernels: 75.4 us -> 117 us
  blocking collectives: 41.5 us -> 0 us
  local copies, waits for them, and re-layouts: 21 us -> 3.51 us
  starting transfers between devices: 14.4 us -> 0 us
  matrix products: 19.6 us -> 10.6 us
  waiting for transfers between devices: 7.22 us -> 0 us
    psum x2 -> x0, blocking collectives: 41.5 us -> none  [the longest x1 23 us: shards(): summed_p, summed_q = lax.psum((partial_product, part_q), 'tensor')]
    pallas_call x0 -> x3, Pallas kernels: none -> 37 us  [the longest x1 20.6 us: exchange(): pl.pallas_call(functools.partial(exchange_kernel, n), out_shape=(jax.Shap...]
    all_to_all x4 -> x0, starting transfers between devices: 14.4 us -> none  [the longest x1 4.21 us: shards(): lax.all_to_all(row_loss_curvature[send_order], 'tenant', split_axis=0, co...]
    scatter x4 -> x0, local copies, waits for them, and re-layouts: 7.31 us -> none  [the longest x1 2.99 us: shards(): grouped_gate = jnp.zeros_like(got_gate).at[arrival].set(got_gate)]
    all_to_all x4 -> x0, waiting for transfers between devices: 7.22 us -> none  [the longest x1 5.43 us: shards(): lax.all_to_all(feats[send_order], 'tenant', split_axis=0, concat_axis=0,...]
    gather x4 -> x0, local copies, waits for them, and re-layouts: 6.62 us -> none  [the longest x1 2.09 us: shards(): gate_preactivation[send_order]]
    pallas_call x1, Pallas kernels: 75.4 us -> 79.5 us  [line_products(): pl.pallas_call(functools.partial(line_kernel, nb, resident, streams), out...]
    dot_general x1, matrix products: 2.98 us -> 0.94 us  [shards(): jnp.einsum('wqh,whx->wqx', lowrank_tangent, adapter_output_factors.astype...]
  transfers between devices with their start and end apart: 4 -> 0, of which waited for: 2 -> 0; matrix products, arithmetic and copies ran while one was open for 10% -> 0% of each run, Pallas kernels for 0% -> 0%
where the time goes in v2:
time: 134 us
  Pallas kernels  117 us (87%)
  matrix products  10.6 us (8%)
  local copies, waits for them, and re-layouts  3.51 us (3%)
  other arithmetic  2.19 us (2%)
    pallas_call x1, Pallas kernels, line_products(): pl.pallas_call(functools.partial(line_kernel, nb, resident, streams), out...  79.5 us
    pallas_call x1, Pallas kernels, exchange(): pl.pallas_call(functools.partial(exchange_kernel, n), out_shape=(jax.Shap...  20.6 us
    pallas_call x2, Pallas kernels, tensor_sum(): pl.pallas_call(sum_kernel, out_shape=jax.ShapeDtypeStruct(x.shape, x.dtyp...  16.5 us
    unnamed x28, local copies, waits for them, and re-layouts  3.51 us
    dot_general x1, matrix products, shards(): jnp.einsum('wqh,whx->wqx', project_rows, iterate_output_factors, precisio...  2.77 us

profile of v2, /device:TPU:0, one launch (start us, length us, event | category | flops | bytes accessed | tf_op | source)
XLA Modules:
  0.0 133.7 jit_solution(15386340871074402167)
XLA Ops:
  0.6 0.0 copy-start
  0.7 0.8 convert_element_type.21
  1.4 0.7 fusion.15
  2.1 0.1 select_select_fusion.meta_ref
  2.3 1.6 %copy.15.gate_ref = bf16[128,3696]{1,0:T(8,128)(2,1)S(1)} copy(bf16[128,3696]{0,1:T(8,128)(2,1)} %param.13) | data formatting | bytes 1892352 | tf_op args[1]
  3.9 20.6 %shard_map.139 = (bf16[128,2048]{1,0:T(8,128)(2,1)S(1)}, bf16[128,3696]{1,0:T(8,128)(2,1)S(1)}, f32[128,1]{1,0:T(8,128)S(1)}) custom-call(bf16[128,2048]{1,0:T(8,128)(2,1)S(1)} %copy-done.2, bf16[128,3696]{1,0:T(8,128)(2,1)S(1)} %copy.15.gate_ref, f32[128,128]{1,0:T(8,128)S(1)} %select_select_fusion.meta_ref), custom_call_target="tpu_custom_call" | custom-call | tf_op jit(solution)/shard_map/pallas_call | solution.py:405
  24.4 0.0 copy-start.1
  24.5 0.0 copy-start.3
  24.5 0.6 fusion.20
  25.1 0.0 copy-done.11
  25.1 0.3 fusion.19
  25.4 0.1 pad_maximum_fusion
  25.5 9.9 %shard_map.140 = f32[128,64]{1,0:T(8,128)S(1)} custom-call(f32[128,64]{1,0:T(8,128)S(1)} %bitcast.25), custom_call_target="tpu_custom_call" | custom-call | tf_op jit(solution)/shard_map/pallas_call | solution.py:287
  35.4 0.9 fusion.8
  36.4 0.5 convert_multiply_fusion
  36.9 1.0 copy-done.4
  37.9 2.8 %fusion.3 = bf16[4,32,3696]{2,1,0:T(8,128)(2,1)} fusion(f32[4,32,3696]{2,1,0:T(8,128)S(1)} %bitcast.27, f32[4,32,3696]{2,1,0:T(8,128)S(1)} %fusion.8, f32[4,32,3696]{2,1,0:T(8,128)S(1)} %copy-done.4, f32[4,32,64]{2,1,0:T(8,128)S(1)} %bitcast.23), kind=kOutput, calls=%fused_computation.5 | convolution fusion | flops 183562240 | bytes 6656000 | tf_op jit(solution)/shard_map/wqh,whx->wqx/dot_general | solution.py:507
  40.7 79.5 %shard_map.141 = (bf16[128,2048]{1,0:T(8,128)(2,1)}, bf16[128,3696]{1,0:T(8,128)(2,1)}) custom-call(bf16[128,3696]{1,0:T(8,128)(2,1)} %bitcast.30, f32[128,1]{1,0:T(8,128)} %copy-done.3, bf16[128,3696]{1,0:T(8,128)(2,1)} %copy-done.1, bf16[3696,8192]{1,0:T(8,128)(2,1)} %weight_ref.1), custom_call_target="tpu_custom_call" | custom-call | flops 15502147584 | bytes 90832896 | tf_op jit(solution)/shard_map/pallas_call | solution.py:225
  120.2 1.7 %fusion.21 = f32[4,32,32]{2,1,0:T(8,128)S(1)} fusion(bf16[4,32,3696]{2,1,0:T(8,128)(2,1)} %bitcast.28, bf16[4,32,3696]{2,1,0:T(8,128)(2,1)S(1)} %copy-done), kind=kOutput, calls=%fused_computation.39 | convolution fusion | flops 30277632 | bytes 1908736 | tf_op jit(solution)/shard_map/acv,apv->acp/dot_general | solution.py:533
  121.9 6.6 %shard_map.142 = f32[128,32]{1,0:T(8,128)S(1)} custom-call(f32[128,32]{1,0:T(8,128)S(1)} %bitcast.26), custom_call_target="tpu_custom_call" | custom-call | tf_op jit(solution)/shard_map/pallas_call | solution.py:287
  128.6 1.7 %fusion.4 = f32[4,2048,32]{1,2,0:T(8,128)} fusion(bf16[4,32,2048]{2,1,0:T(8,128)(2,1)S(1)} %bitcast.21, f32[4,32,32]{2,1,0:T(8,128)S(1)} %bitcast.31, f32[4,2048,32]{1,2,0:T(8,128)S(1)} %copy-done.10, f32[4,2048,32]{1,2,0:T(8,128)S(1)} %copy-done.7), kind=kOutput, calls=%fused_computation.7 | convolution fusion | flops 101711872 | bytes 3686400 | tf_op jit(solution)/shard_map/tsd,tsr->tdr/dot_general | solution.py:543
  130.3 0.0 copy-done.8
  130.4 2.5 %fusion = f32[4,32,3696]{2,1,0:T(8,128)} fusion(bf16[4,32,3696]{2,1,0:T(8,128)(2,1)S(1)} %bitcast.29, f32[4,32,3696]{2,1,0:T(8,128)S(1)} %copy-done.9, f32[4,32,3696]{2,1,0:T(8,128)S(1)} %copy-done.5, f32[4,32,64]{2,1,0:T(8,128)S(1)} %bitcast.24), kind=kOutput, calls=%fused_computation.1 | convolution fusion | flops 183562240 | bytes 6656000 | tf_op jit(solution)/shard_map/bji,bjw->biw/dot_general | solution.py:546
  132.9 0.8 copy.21
  (23 shorter events, 0.1 us)
Async XLA Ops:
  0.6 34.8 %copy-start = (bf16[4,32,3696]{2,1,0:T(8,128)(2,1)S(1)}, bf16[4,32,3696]{2,1,0:T(8,128)(2,1)}, u32[]{:S(2)}) copy-start(bf16[4,32,3696]{2,1,0:T(8,128)(2,1)} %param.19) | copy-start | bytes 2838532
  0.6 3.2 %copy-start.2 = (bf16[128,2048]{1,0:T(8,128)(2,1)S(1)}, bf16[128,2048]{1,0:T(8,128)(2,1)}, u32[]{:S(2)}) copy-start(bf16[128,2048]{1,0:T(8,128)(2,1)} %x_ref.1) | copy-start | bytes 1572868
  3.9 20.6 %copy-start.6 = (f32[4,2048,32]{1,2,0:T(8,128)S(1)}, f32[4,2048,32]{1,2,0:T(8,128)}, u32[]{:S(2)}) copy-start(f32[4,2048,32]{1,2,0:T(8,128)} %param.20) | copy-start | bytes 3145732
  3.9 21.3 %copy-start.11 = (bf16[4,2048,32]{1,2,0:T(8,128)(2,1)S(1)}, bf16[4,2048,32]{1,2,0:T(8,128)(2,1)}, u32[]{:S(2)}) copy-start(bf16[4,2048,32]{1,2,0:T(8,128)(2,1)} %param.18) | copy-start | bytes 1572868
  24.4 11.9 %copy-start.1 = (bf16[128,3696]{1,0:T(8,128)(2,1)}, bf16[128,3696]{1,0:T(8,128)(2,1)S(1)}, u32[]{:S(2)}) copy-start(bf16[128,3696]{1,0:T(8,128)(2,1)S(1)} %get-tuple-element.9.gate_ref) | copy-start | bytes 2838532
  24.5 11.9 %copy-start.3 = (f32[128,1]{1,0:T(8,128)}, f32[128,1]{1,0:T(8,128)S(1)}, u32[]{:S(2)}) copy-start(f32[128,1]{1,0:T(8,128)S(1)} %get-tuple-element.10.w_ref) | copy-start | bytes 1540
  36.4 1.5 %copy-start.4 = (f32[4,32,3696]{2,1,0:T(8,128)S(1)}, f32[4,32,3696]{2,1,0:T(8,128)}, u32[]{:S(2)}) copy-start(f32[4,32,3696]{2,1,0:T(8,128)} %param.21) | copy-start | bytes 5677060
  40.7 87.9 %copy-start.10 = (f32[4,2048,32]{1,2,0:T(8,128)S(1)}, f32[4,2048,32]{1,2,0:T(8,128)}, u32[]{:S(2)}) copy-start(f32[4,2048,32]{1,2,0:T(8,128)} %param.22) | copy-start | bytes 3145732
  120.2 8.4 %copy-start.7 = (f32[4,2048,32]{1,2,0:T(8,128)S(1)}, f32[4,2048,32]{1,2,0:T(8,128)}, u32[]{:S(2)}) copy-start(f32[4,2048,32]{1,2,0:T(8,128)} %param.20) | copy-start | bytes 3145732
  120.2 10.1 %copy-start.9 = (f32[4,32,3696]{2,1,0:T(8,128)S(1)}, f32[4,32,3696]{2,1,0:T(8,128)}, u32[]{:S(2)}) copy-start(f32[4,32,3696]{2,1,0:T(8,128)} %param.23) | copy-start | bytes 5677060
  128.5 1.8 %copy-start.5 = (f32[4,32,3696]{2,1,0:T(8,128)S(1)}, f32[4,32,3696]{2,1,0:T(8,128)}, u32[]{:S(2)}) copy-start(f32[4,32,3696]{2,1,0:T(8,128)} %param.21) | copy-start | bytes 5677060
  128.6 1.8 %copy-start.8 = (bf16[128,3696]{1,0:T(8,128)(2,1)S(1)}, bf16[128,3696]{1,0:T(8,128)(2,1)}, u32[]{:S(2)}) copy-start(bf16[128,3696]{1,0:T(8,128)(2,1)} %get-tuple-element.11) | copy-start | bytes 2838532
  130.4 2.5 %copy-start.12 = (bf16[128,2048]{1,0:T(8,128)(2,1)S(1)}, bf16[128,2048]{1,0:T(8,128)(2,1)}, u32[]{:S(2)}) copy-start(bf16[128,2048]{1,0:T(8,128)(2,1)} %get-tuple-element.22) | copy-start | bytes 1572868

commit v3 on v2

--- a/solution.py
+++ b/solution.py
@@ -17,7 +17,7 @@
 
 
 LINE = 4
-COLS = 256
+COLS = 128
 MESH = pl.DeviceIdType.MESH
 
 
@@ -153,11 +153,9 @@
             slot = jnp.where(u < 0, i, resident + jnp.maximum(u, 0) % streams)
             for q in range(n):
                 fetch(slot, i, q).wait()
-                y[i, q] = jnp.dot(
-                    h_ref[...],
-                    wbuf[slot, :, q * COLS : (q + 1) * COLS],
-                    preferred_element_type=jnp.float32,
-                )
+            product = jnp.dot(h_ref[...], wbuf[slot], preferred_element_type=jnp.float32)
+            for q in range(n):
+                y[i, q] = product[:, q * COLS : (q + 1) * COLS]
             refill(u)
 
         @pl.when(i >= last_lag)
@@ -218,7 +216,7 @@
     rows, hidden = hidden_tan.shape
     width = weight.shape[1]
     nb = width // (LINE * COLS)
-    resident, streams = 3, 2
+    resident, streams = 6, 4
     bf16, f32 = jnp.bfloat16, jnp.float32
     vmem = pl.BlockSpec(memory_space=pltpu.VMEM)
     sems = pltpu.SemaphoreType.DMA
@@ -452,6 +450,7 @@
         and per_dest % 16 == 0
         and f_local % 16 == 0
         and down_projection_weight.shape[1] % (LINE * COLS) == 0
+        and down_projection_weight.shape[1] >= 12 * LINE * COLS
     )
     if by_kernels:
         grouped_input_rows, grouped_gate, weights = exchange(

time: 134 us -> 139 us (1.037)
  Pallas kernels: 117 us -> 122 us
    pallas_call x1, Pallas kernels: 79.5 us -> 85.2 us  [line_products(): pl.pallas_call(functools.partial(line_kernel, nb, resident, streams), out...]
where the time goes in v3:
time: 139 us
  Pallas kernels  122 us (88%)
  matrix products  10.6 us (8%)
  local copies, waits for them, and re-layouts  3.51 us (3%)
  other arithmetic  2.19 us (2%)
    pallas_call x1, Pallas kernels, line_products(): pl.pallas_call(functools.partial(line_kernel, nb, resident, streams), out...  85.2 us
    pallas_call x1, Pallas kernels, exchange(): pl.pallas_call(functools.partial(exchange_kernel, n), out_shape=(jax.Shap...  20.6 us
    pallas_call x2, Pallas kernels, tensor_sum(): pl.pallas_call(sum_kernel, out_shape=jax.ShapeDtypeStruct(x.shape, x.dtyp...  16.2 us
    unnamed x28, local copies, waits for them, and re-layouts  3.51 us

profile of v3, /device:TPU:0, one launch (start us, length us, event | category | flops | bytes accessed | tf_op | source)
XLA Modules:
  0.0 139.2 jit_solution(18324725562276931687)
XLA Ops:
  0.6 0.0 copy-start
  0.7 0.8 convert_element_type.21
  1.4 0.7 fusion.15
  2.1 0.1 select_select_fusion.meta_ref
  2.3 1.6 %copy.15.gate_ref = bf16[128,3696]{1,0:T(8,128)(2,1)S(1)} copy(bf16[128,3696]{0,1:T(8,128)(2,1)} %param.13) | data formatting | bytes 1892352 | tf_op args[1]
  3.9 0.0 copy-start.11
  3.9 20.6 %shard_map.139 = (bf16[128,2048]{1,0:T(8,128)(2,1)S(1)}, bf16[128,3696]{1,0:T(8,128)(2,1)S(1)}, f32[128,1]{1,0:T(8,128)S(1)}) custom-call(bf16[128,2048]{1,0:T(8,128)(2,1)S(1)} %copy-done.2, bf16[128,3696]{1,0:T(8,128)(2,1)S(1)} %copy.15.gate_ref, f32[128,128]{1,0:T(8,128)S(1)} %select_select_fusion.meta_ref), custom_call_target="tpu_custom_call" | custom-call | tf_op jit(solution)/shard_map/pallas_call | solution.py:403
  24.5 0.0 copy-start.3
  24.5 0.6 fusion.20
  25.1 0.0 copy-done.11
  25.1 0.3 fusion.19
  25.4 0.1 pad_maximum_fusion
  25.5 9.9 %shard_map.140 = f32[128,64]{1,0:T(8,128)S(1)} custom-call(f32[128,64]{1,0:T(8,128)S(1)} %bitcast.25), custom_call_target="tpu_custom_call" | custom-call | tf_op jit(solution)/shard_map/pallas_call | solution.py:285
  35.4 1.0 fusion.8
  36.4 0.5 convert_multiply_fusion
  36.9 1.0 copy-done.4
  37.9 2.8 %fusion.3 = bf16[4,32,3696]{2,1,0:T(8,128)(2,1)} fusion(f32[4,32,3696]{2,1,0:T(8,128)S(1)} %bitcast.27, f32[4,32,3696]{2,1,0:T(8,128)S(1)} %fusion.8, f32[4,32,3696]{2,1,0:T(8,128)S(1)} %copy-done.4, f32[4,32,64]{2,1,0:T(8,128)S(1)} %bitcast.23), kind=kOutput, calls=%fused_computation.5 | convolution fusion | flops 183562240 | bytes 6656000 | tf_op jit(solution)/shard_map/wqh,whx->wqx/dot_general | solution.py:506
  40.7 85.2 %shard_map.141 = (bf16[128,2048]{1,0:T(8,128)(2,1)}, bf16[128,3696]{1,0:T(8,128)(2,1)}) custom-call(bf16[128,3696]{1,0:T(8,128)(2,1)} %bitcast.30, f32[128,1]{1,0:T(8,128)} %copy-done.3, bf16[128,3696]{1,0:T(8,128)(2,1)} %copy-done.1, bf16[3696,8192]{1,0:T(8,128)(2,1)} %weight_ref.1), custom_call_target="tpu_custom_call" | custom-call | flops 15502147584 | bytes 90832896 | tf_op jit(solution)/shard_map/pallas_call | solution.py:223
  125.9 1.7 %fusion.21 = f32[4,32,32]{2,1,0:T(8,128)S(1)} fusion(bf16[4,32,3696]{2,1,0:T(8,128)(2,1)} %bitcast.28, bf16[4,32,3696]{2,1,0:T(8,128)(2,1)S(1)} %copy-done), kind=kOutput, calls=%fused_computation.39 | convolution fusion | flops 30277632 | bytes 1908736 | tf_op jit(solution)/shard_map/acv,apv->acp/dot_general | solution.py:532
  127.7 6.3 %shard_map.142 = f32[128,32]{1,0:T(8,128)S(1)} custom-call(f32[128,32]{1,0:T(8,128)S(1)} %bitcast.26), custom_call_target="tpu_custom_call" | custom-call | tf_op jit(solution)/shard_map/pallas_call | solution.py:285
  134.0 1.7 %fusion.4 = f32[4,2048,32]{1,2,0:T(8,128)} fusion(bf16[4,32,2048]{2,1,0:T(8,128)(2,1)S(1)} %bitcast.21, f32[4,32,32]{2,1,0:T(8,128)S(1)} %bitcast.31, f32[4,2048,32]{1,2,0:T(8,128)S(1)} %copy-done.10, f32[4,2048,32]{1,2,0:T(8,128)S(1)} %copy-done.7), kind=kOutput, calls=%fused_computation.7 | convolution fusion | flops 101711872 | bytes 3686400 | tf_op jit(solution)/shard_map/tsd,tsr->tdr/dot_general | solution.py:542
  135.8 0.0 copy-done.8
  135.8 2.5 %fusion = f32[4,32,3696]{2,1,0:T(8,128)} fusion(bf16[4,32,3696]{2,1,0:T(8,128)(2,1)S(1)} %bitcast.29, f32[4,32,3696]{2,1,0:T(8,128)S(1)} %copy-done.9, f32[4,32,3696]{2,1,0:T(8,128)S(1)} %copy-done.5, f32[4,32,64]{2,1,0:T(8,128)S(1)} %bitcast.24), kind=kOutput, calls=%fused_computation.1 | convolution fusion | flops 183562240 | bytes 6656000 | tf_op jit(solution)/shard_map/bji,bjw->biw/dot_general | solution.py:545
  138.4 0.8 copy.21
  (23 shorter events, 0.1 us)
Async XLA Ops:
  0.6 34.8 %copy-start = (bf16[4,32,3696]{2,1,0:T(8,128)(2,1)S(1)}, bf16[4,32,3696]{2,1,0:T(8,128)(2,1)}, u32[]{:S(2)}) copy-start(bf16[4,32,3696]{2,1,0:T(8,128)(2,1)} %param.19) | copy-start | bytes 2838532
  0.6 3.2 %copy-start.2 = (bf16[128,2048]{1,0:T(8,128)(2,1)S(1)}, bf16[128,2048]{1,0:T(8,128)(2,1)}, u32[]{:S(2)}) copy-start(bf16[128,2048]{1,0:T(8,128)(2,1)} %x_ref.1) | copy-start | bytes 1572868
  3.9 20.6 %copy-start.6 = (f32[4,2048,32]{1,2,0:T(8,128)S(1)}, f32[4,2048,32]{1,2,0:T(8,128)}, u32[]{:S(2)}) copy-start(f32[4,2048,32]{1,2,0:T(8,128)} %param.20) | copy-start | bytes 3145732
  3.9 21.3 %copy-start.11 = (bf16[4,2048,32]{1,2,0:T(8,128)(2,1)S(1)}, bf16[4,2048,32]{1,2,0:T(8,128)(2,1)}, u32[]{:S(2)}) copy-start(bf16[4,2048,32]{1,2,0:T(8,128)(2,1)} %param.18) | copy-start | bytes 1572868
  24.5 11.9 %copy-start.1 = (bf16[128,3696]{1,0:T(8,128)(2,1)}, bf16[128,3696]{1,0:T(8,128)(2,1)S(1)}, u32[]{:S(2)}) copy-start(bf16[128,3696]{1,0:T(8,128)(2,1)S(1)} %get-tuple-element.9.gate_ref) | copy-start | bytes 2838532
  24.5 11.9 %copy-start.3 = (f32[128,1]{1,0:T(8,128)}, f32[128,1]{1,0:T(8,128)S(1)}, u32[]{:S(2)}) copy-start(f32[128,1]{1,0:T(8,128)S(1)} %get-tuple-element.10.w_ref) | copy-start | bytes 1540
  36.4 1.5 %copy-start.4 = (f32[4,32,3696]{2,1,0:T(8,128)S(1)}, f32[4,32,3696]{2,1,0:T(8,128)}, u32[]{:S(2)}) copy-start(f32[4,32,3696]{2,1,0:T(8,128)} %param.21) | copy-start | bytes 5677060
  40.7 93.3 %copy-start.10 = (f32[4,2048,32]{1,2,0:T(8,128)S(1)}, f32[4,2048,32]{1,2,0:T(8,128)}, u32[]{:S(2)}) copy-start(f32[4,2048,32]{1,2,0:T(8,128)} %param.22) | copy-start | bytes 3145732
  125.9 8.1 %copy-start.7 = (f32[4,2048,32]{1,2,0:T(8,128)S(1)}, f32[4,2048,32]{1,2,0:T(8,128)}, u32[]{:S(2)}) copy-start(f32[4,2048,32]{1,2,0:T(8,128)} %param.20) | copy-start | bytes 3145732
  125.9 9.9 %copy-start.9 = (f32[4,32,3696]{2,1,0:T(8,128)S(1)}, f32[4,32,3696]{2,1,0:T(8,128)}, u32[]{:S(2)}) copy-start(f32[4,32,3696]{2,1,0:T(8,128)} %param.23) | copy-start | bytes 5677060
  134.0 1.8 %copy-start.5 = (f32[4,32,3696]{2,1,0:T(8,128)S(1)}, f32[4,32,3696]{2,1,0:T(8,128)}, u32[]{:S(2)}) copy-start(f32[4,32,3696]{2,1,0:T(8,128)} %param.21) | copy-start | bytes 5677060
  134.0 1.8 %copy-start.8 = (bf16[128,3696]{1,0:T(8,128)(2,1)S(1)}, bf16[128,3696]{1,0:T(8,128)(2,1)}, u32[]{:S(2)}) copy-start(bf16[128,3696]{1,0:T(8,128)(2,1)} %get-tuple-element.11) | copy-start | bytes 2838532
  135.8 2.5 %copy-start.12 = (bf16[128,2048]{1,0:T(8,128)(2,1)S(1)}, bf16[128,2048]{1,0:T(8,128)(2,1)}, u32[]{:S(2)}) copy-start(bf16[128,2048]{1,0:T(8,128)(2,1)} %get-tuple-element.22) | copy-start | bytes 1572868
